TPU v7x, 256 devices: a whole 4x4x8 slice. The times are simulated.
256 devices in a mesh: ctx: 64 (over z, x, core), head: 4 (over y).
Axes of the slice: x: 4, y: 4, z: 8, core: 2. Of those that a mesh axis runs over, the one named last changes fastest.
Arguments:
- queries: bfloat16 [49152, 4096], P('ctx', 'head'), may hold values from -20 to 20
- keys: bfloat16 [49152, 4096], P('ctx', 'head'), may hold values from -6 to 6
- values: bfloat16 [49152, 4096], P('ctx', 'head'), may hold values from -64 to 64
- cotangent: bfloat16 [49152, 4096], P('ctx', 'head'), may hold values from -6 to 6
- state_in: float32 [32, 128, 128], P('head'), may hold values from -96 to 96
Outputs:
- output: bfloat16 [49152, 4096], P('ctx', 'head')
- grad_queries: bfloat16 [49152, 4096], P('ctx', 'head')
- grad_keys: bfloat16 [49152, 4096], P('ctx', 'head')
- grad_values: bfloat16 [49152, 4096], P('ctx', 'head')
All inputs are finite; a program needn't handle non-finite values.
Results may differ from a plain program's by a relative error of at most 0.0058.
Values sent between devices are 32-bit elements; how exact they have to be, the bound alone decides.
A program may use at most 128 MiB of HBM per device.

v0:
```python
import jax
import jax.numpy as jnp
from jax import lax
from jax.sharding import PartitionSpec as P

HEADS = 32
DH = 128


def shifted(block, axis, distance):
    devices = range(lax.axis_size(axis))
    route = [(i - distance, i) for i in devices if i - distance in devices]
    return lax.ppermute(block, axis, route)


def causal_scores(left, right, causal_mask):
    scores = jnp.einsum("thi,shi->hts", left, right, preferred_element_type=jnp.float32)
    return jnp.where(causal_mask[None], scores, 0.0).astype(jnp.bfloat16)


def earlier_forward(local_term):
    total = local_term
    distance = 1
    while distance < lax.axis_size("ctx"):
        total = total + shifted(total, "ctx", distance)
        distance = distance * 2
    return total - local_term


def later_backward(local_term):
    total = local_term
    distance = 1
    while distance < lax.axis_size("ctx"):
        total = total + shifted(total, "ctx", -distance)
        distance = distance * 2
    return total - local_term


def local(queries, keys, values, cotangent, state_in):
    tok_count = queries.shape[0]
    heads_here = queries.shape[1] // DH
    feat_here = heads_here * DH
    feat_count = HEADS * DH
    query_heads = queries.reshape(tok_count, heads_here, DH)
    key_heads = keys.reshape(tok_count, heads_here, DH)
    value_heads = values.reshape(tok_count, heads_here, DH)
    positions = jnp.arange(tok_count)
    causal_mask = positions[:, None] >= positions[None, :]
    kv_local = jnp.einsum(
        "shi,she->hie", key_heads, value_heads, preferred_element_type=jnp.float32
    )
    prefix = earlier_forward(kv_local)
    state_low = (state_in + prefix).astype(jnp.bfloat16)
    forward_scores = causal_scores(query_heads, key_heads, causal_mask)
    attention = jnp.einsum(
        "hts,she->the", forward_scores, value_heads, preferred_element_type=jnp.float32
    )
    attention = attention + jnp.einsum(
        "thi,hie->the", query_heads, state_low, preferred_element_type=jnp.float32
    )
    attention = attention.reshape(tok_count, feat_here)
    grad_float = cotangent.astype(jnp.float32)
    sum_squares, cross_sum = lax.psum(
        (jnp.sum(attention * attention, axis=1), jnp.sum(grad_float * attention, axis=1)), "head"
    )
    inverse_rms = lax.rsqrt(sum_squares / feat_count + 1e-06)
    output = (attention * inverse_rms[:, None]).astype(jnp.bfloat16)
    grad_attention = (
        inverse_rms[:, None] * grad_float
        - attention * (inverse_rms**3 * cross_sum / feat_count)[:, None]
    ).astype(jnp.bfloat16)
    grad_heads = grad_attention.reshape(tok_count, heads_here, DH)
    qd_local = jnp.einsum(
        "thi,the->hie", query_heads, grad_heads, preferred_element_type=jnp.float32
    )
    later_sum = later_backward(qd_local)
    suffix_low = later_sum.astype(jnp.bfloat16)
    grad_scores = causal_scores(grad_heads, value_heads, causal_mask)
    grad_query = jnp.einsum(
        "hts,shi->thi", grad_scores, key_heads, preferred_element_type=jnp.float32
    )
    grad_query = grad_query + jnp.einsum(
        "the,hie->thi", grad_heads, state_low, preferred_element_type=jnp.float32
    )
    grad_key = jnp.einsum(
        "hts,thi->shi", grad_scores, query_heads, preferred_element_type=jnp.float32
    )
    grad_key = grad_key + jnp.einsum(
        "she,hie->shi", value_heads, suffix_low, preferred_element_type=jnp.float32
    )
    grad_value = jnp.einsum(
        "hts,the->she", forward_scores, grad_heads, preferred_element_type=jnp.float32
    )
    grad_value = grad_value + jnp.einsum(
        "shi,hie->she", key_heads, suffix_low, preferred_element_type=jnp.float32
    )
    return (
        output,
        grad_query.reshape(tok_count, feat_here).astype(jnp.bfloat16),
        grad_key.reshape(tok_count, feat_here).astype(jnp.bfloat16),
        grad_value.reshape(tok_count, feat_here).astype(jnp.bfloat16),
    )


def solution(mesh):
    in_specs = (
        P("ctx", "head"),
        P("ctx", "head"),
        P("ctx", "head"),
        P("ctx", "head"),
        P("head", None, None),
    )
    out_specs = (P("ctx", "head"), P("ctx", "head"), P("ctx", "head"), P("ctx", "head"))
    return jax.shard_map(local, mesh=mesh, in_specs=in_specs, out_specs=out_specs, check_vma=False)
```

profile of v0, /device:TPU:65, one launch (start us, length us, event | category | flops | bytes accessed | tf_op | source)
XLA Modules:
  0.0 302.2 jit_solution(16070962470593752834)
XLA Ops:
  12.4 6.1 %collective-permute-done = f32[8,128,128]{2,1,0:T(8,128)S(1)} collective-permute-done((f32[8,128,128]{2,1,0:T(8,128)S(1)}, f32[8,128,128]{2,1,0:T(8,128)S(1)}, u32[]{:S(2)}, u32[]{:S(2)}) %collective-permute-start) | collective-permute-done | bytes 524320 | tf_op jit(solution)/shard_map/ppermute | solution.py:13
  21.7 10.8 %collective-permute-done.1 = f32[8,128,128]{2,1,0:T(8,128)S(1)} collective-permute-done((f32[8,128,128]{2,1,0:T(8,128)S(1)}, f32[8,128,128]{2,1,0:T(8,128)S(1)}, u32[]{:S(2)}, u32[]{:S(2)}) %collective-permute-start.1) | collective-permute-done | bytes 524320 | tf_op jit(solution)/shard_map/ppermute | solution.py:13
  32.6 4.2 %collective-permute-start.2 = (f32[8,128,128]{2,1,0:T(8,128)S(1)}, f32[8,128,128]{2,1,0:T(8,128)S(1)}, u32[]{:S(2)}, u32[]{:S(2)}) collective-permute-start(f32[8,128,128]{2,1,0:T(8,128)S(1)} %add.63), channel_id=1, source_target_pairs={{0,16},{4,20},{8,24},{12,28},{16,32},{20,36},{24,40},{28,44},{32,4... | collective-permute-start | bytes 1572872 | tf_op jit(solution)/shard_map/ppermute | solution.py:13
  36.8 9.2 %collective-permute-done.2 = f32[8,128,128]{2,1,0:T(8,128)S(1)} collective-permute-done((f32[8,128,128]{2,1,0:T(8,128)S(1)}, f32[8,128,128]{2,1,0:T(8,128)S(1)}, u32[]{:S(2)}, u32[]{:S(2)}) %collective-permute-start.2) | collective-permute-done | bytes 524320 | tf_op jit(solution)/shard_map/ppermute | solution.py:13
  46.1 7.4 %collective-permute-start.3 = (f32[8,128,128]{2,1,0:T(8,128)S(1)}, f32[8,128,128]{2,1,0:T(8,128)S(1)}, u32[]{:S(2)}, u32[]{:S(2)}) collective-permute-start(f32[8,128,128]{2,1,0:T(8,128)S(1)} %add.64), channel_id=1, source_target_pairs={{0,32},{4,36},{8,40},{12,44},{16,48},{20,52},{24,56},{28,60},{32,6... | collective-permute-start | bytes 1572872 | tf_op jit(solution)/shard_map/ppermute | solution.py:13
  53.7 9.4 %collective-permute-done.3 = f32[8,128,128]{2,1,0:T(8,128)S(1)} collective-permute-done((f32[8,128,128]{2,1,0:T(8,128)S(1)}, f32[8,128,128]{2,1,0:T(8,128)S(1)}, u32[]{:S(2)}, u32[]{:S(2)}) %collective-permute-start.3) | collective-permute-done | bytes 524320 | tf_op jit(solution)/shard_map/ppermute | solution.py:13
  68.2 8.8 %collective-permute-done.4 = f32[8,128,128]{2,1,0:T(8,128)S(1)} collective-permute-done((f32[8,128,128]{2,1,0:T(8,128)S(1)}, f32[8,128,128]{2,1,0:T(8,128)S(1)}, u32[]{:S(2)}, u32[]{:S(2)}) %collective-permute-start.4) | collective-permute-done | bytes 524320 | tf_op jit(solution)/shard_map/ppermute | solution.py:13
  80.0 6.3 %fusion.5 = f32[8,768,128]{1,2,0:T(8,128)} fusion(bf16[8,768,768]{2,1,0:T(8,128)(2,1)S(1)} %select_convert_fusion.1, bf16[768,1024]{1,0:T(8,128)(2,1)} %param.7), kind=kOutput, calls=%fused_computation.16 | convolution fusion | flops 1207959552 | bytes 14155776 | tf_op jit(solution)/shard_map/hts,she->the/dot_general | solution.py:55
  86.3 26.3 %collective-permute-done.5 = f32[8,128,128]{2,1,0:T(8,128)} collective-permute-done((f32[8,128,128]{2,1,0:T(8,128)}, f32[8,128,128]{2,1,0:T(8,128)}, u32[]{:S(2)}, u32[]{:S(2)}) %collective-permute-start.5) | collective-permute-done | bytes 524320 | tf_op jit(solution)/shard_map/ppermute | solution.py:13
  114.2 4.3 %multiply_reduce_fusion = (f32[768]{0:T(1024)S(1)}, f32[768,8,128]{0,2,1:T(8,128)}) fusion(bf16[8,128,128]{2,1,0:T(8,128)(2,1)S(1)} %add_convert_fusion.1, f32[8,768,128]{1,2,0:T(8,128)} %fusion.5, bf16[768,1024]{1,0:T(8,128)(2,1)S(1)} %copy-done), kind=kOutput, calls=%fused_computation.14 | convolution fusion | flops 203685120 | bytes 8129536 | tf_op jit(solution)/shard_map/thi,hie->the/dot_general | solution.py:58
  124.5 8.8 %all-reduce = (f32[768]{0:T(1024)S(1)}, f32[768]{0:T(1024)S(1)}) all-reduce(f32[768]{0:T(1024)S(1)} %get-tuple-element.14, f32[768]{0:T(1024)S(1)} %fusion.2), channel_id=1, replica_groups=mesh['ctx'=64,'head'=4] {'head'}, use_global_device_ids=true, to_apply=%region_1.2 | all-reduce | flops 1536 | bytes 12288 | tf_op jit(solution)/shard_map/psum | solution.py:63
  133.3 4.2 %fusion.1 = (bf16[768,1024]{1,0:T(8,128)(2,1)}, bf16[768,1024]{1,0:T(8,128)(2,1)}) fusion(bf16[768,1024]{1,0:T(8,128)(2,1)S(1)} %copy-done.8, f32[768,1024]{1,0:T(8,128)} %copy.16, f32[768]{0:T(1024)S(1)} %get-tuple-element.12, f32[768]{0:T(1024)S(1)} %get-tuple-element.13), kind=kLoop, calls=%fused_computation.5 | loop fusion | flops 5505024 | bytes 7870464 | tf_op jit(solution)/shard_map/convert_element_type | solution.py:71
  139.9 4.5 %collective-permute-start.6 = (f32[8,128,128]{1,2,0:T(8,128)S(1)}, f32[8,128,128]{1,2,0:T(8,128)S(1)}, u32[]{:S(2)}, u32[]{:S(2)}) collective-permute-start(f32[8,128,128]{1,2,0:T(8,128)S(1)} %fusion.21), channel_id=1, source_target_pairs={{4,0},{8,4},{12,8},{16,12},{20,16},{24,20},{28,24},{32,28},{36,32}... | collective-permute-start | bytes 1572872 | tf_op jit(solution)/shard_map/ppermute | solution.py:13
  144.4 8.3 %collective-permute-done.6 = f32[8,128,128]{1,2,0:T(8,128)S(1)} collective-permute-done((f32[8,128,128]{1,2,0:T(8,128)S(1)}, f32[8,128,128]{1,2,0:T(8,128)S(1)}, u32[]{:S(2)}, u32[]{:S(2)}) %collective-permute-start.6) | collective-permute-done | bytes 524320 | tf_op jit(solution)/shard_map/ppermute | solution.py:13
  152.8 12.0 %collective-permute-start.7 = (f32[8,128,128]{1,2,0:T(8,128)S(1)}, f32[8,128,128]{1,2,0:T(8,128)S(1)}, u32[]{:S(2)}, u32[]{:S(2)}) collective-permute-start(f32[8,128,128]{1,2,0:T(8,128)S(1)} %add.73), channel_id=1, source_target_pairs={{8,0},{12,4},{16,8},{20,12},{24,16},{28,20},{32,24},{36,28},{40,32... | collective-permute-start | bytes 1572872 | tf_op jit(solution)/shard_map/ppermute | solution.py:13
  164.8 9.8 %collective-permute-done.7 = f32[8,128,128]{1,2,0:T(8,128)S(1)} collective-permute-done((f32[8,128,128]{1,2,0:T(8,128)S(1)}, f32[8,128,128]{1,2,0:T(8,128)S(1)}, u32[]{:S(2)}, u32[]{:S(2)}) %collective-permute-start.7) | collective-permute-done | bytes 524320 | tf_op jit(solution)/shard_map/ppermute | solution.py:13
  175.5 10.6 %collective-permute-start.8 = (f32[8,128,128]{1,2,0:T(8,128)}, f32[8,128,128]{1,2,0:T(8,128)}, u32[]{:S(2)}, u32[]{:S(2)}) collective-permute-start(f32[8,128,128]{1,2,0:T(8,128)} %add.74), channel_id=1, source_target_pairs={{16,0},{20,4},{24,8},{28,12},{32,16},{36,20},{40,24},{44,28},{48,3... | collective-permute-start | bytes 1572872 | tf_op jit(solution)/shard_map/ppermute | solution.py:13
  186.1 4.1 %select_convert_fusion = bf16[8,768,768]{2,1,0:T(8,128)(2,1)S(1)} fusion(pred[768,768]{1,0:T(8,128)(4,1)} %copy-done.12, bf16[768,8,128]{0,2,1:T(8,128)(2,1)S(1)} %bitcast.104, bf16[768,1024]{1,0:T(8,128)(2,1)S(1)} %copy-done.4), kind=kOutput, calls=%fused_computation | convolution fusion | flops 1217396736 | bytes 13172736 | tf_op jit(solution)/shard_map/thi,shi->hts/dot_general | solution.py:17
  190.2 5.9 %collective-permute-done.8 = f32[8,128,128]{1,2,0:T(8,128)} collective-permute-done((f32[8,128,128]{1,2,0:T(8,128)}, f32[8,128,128]{1,2,0:T(8,128)}, u32[]{:S(2)}, u32[]{:S(2)}) %collective-permute-start.8) | collective-permute-done | bytes 524320 | tf_op jit(solution)/shard_map/ppermute | solution.py:13
  198.2 8.5 %collective-permute-start.9 = (f32[8,128,128]{1,2,0:T(8,128)}, f32[8,128,128]{1,2,0:T(8,128)}, u32[]{:S(2)}, u32[]{:S(2)}) collective-permute-start(f32[8,128,128]{1,2,0:T(8,128)} %add.75), channel_id=1, source_target_pairs={{32,0},{36,4},{40,8},{44,12},{48,16},{52,20},{56,24},{60,28},{64,3... | collective-permute-start | bytes 1572872 | tf_op jit(solution)/shard_map/ppermute | solution.py:13
  206.7 6.2 %fusion.34 = f32[8,768,128]{1,2,0:T(8,128)} fusion(bf16[8,768,768]{2,1,0:T(8,128)(2,1)S(1)} %select_convert_fusion, bf16[768,8,128]{0,2,1:T(8,128)(2,1)} %copy.12), kind=kOutput, calls=%fused_computation.47 | convolution fusion | flops 1207959552 | bytes 14155776 | tf_op jit(solution)/shard_map/hts,shi->thi/dot_general | solution.py:79
  223.9 5.1 %fusion.35 = f32[8,128,768]{2,1,0:T(8,128)S(1)} fusion(bf16[768,8,128]{0,2,1:T(8,128)(2,1)S(1)} %bitcast.106, bf16[8,768,768]{2,1,0:T(8,128)(2,1)} %copy-done.2), kind=kOutput, calls=%fused_computation.48 | convolution fusion | flops 1207959552 | bytes 14155776 | tf_op jit(solution)/shard_map/hts,the->she/dot_general | solution.py:91
  229.0 33.3 %collective-permute-done.10 = f32[8,128,128]{1,2,0:T(8,128)S(1)} collective-permute-done((f32[8,128,128]{1,2,0:T(8,128)S(1)}, f32[8,128,128]{1,2,0:T(8,128)S(1)}, u32[]{:S(2)}, u32[]{:S(2)}) %collective-permute-start.10) | collective-permute-done | bytes 524320 | tf_op jit(solution)/shard_map/ppermute | solution.py:13
  267.1 24.3 %collective-permute-done.11 = f32[8,128,128]{1,2,0:T(8,128)S(1)} collective-permute-done((f32[8,128,128]{1,2,0:T(8,128)S(1)}, f32[8,128,128]{1,2,0:T(8,128)S(1)}, u32[]{:S(2)}, u32[]{:S(2)}) %collective-permute-start.11) | collective-permute-done | bytes 524320 | tf_op jit(solution)/shard_map/ppermute | solution.py:13
  (69 shorter events, 62.7 us)
Async XLA Ops:
  0.6 64.5 %copy-start = (bf16[768,1024]{1,0:T(8,128)(2,1)S(1)}, bf16[768,1024]{1,0:T(8,128)(2,1)}, u32[]{:S(2)}) copy-start(bf16[768,1024]{1,0:T(8,128)(2,1)} %param.5) | copy-start | bytes 4718596
  8.7 23.9 %copy-start.11 = (f32[8,128,128]{2,1,0:T(8,128)}, f32[8,128,128]{2,1,0:T(8,128)S(1)}, u32[]{:S(2)}) copy-start(f32[8,128,128]{2,1,0:T(8,128)S(1)} %fusion.9) | copy-start | bytes 1572868
  8.7 9.8 %collective-permute-start = (f32[8,128,128]{2,1,0:T(8,128)S(1)}, f32[8,128,128]{2,1,0:T(8,128)S(1)}, u32[]{:S(2)}, u32[]{:S(2)}) collective-permute-start(f32[8,128,128]{2,1,0:T(8,128)S(1)} %fusion.9), channel_id=1, source_target_pairs={{0,4},{4,8},{8,12},{12,16},{16,20},{20,24},{24,28},{28,32},{32,36}... | collective-permute-start | bytes 1572872 | tf_op jit(solution)/shard_map/ppermute | solution.py:13
  18.6 13.9 %collective-permute-start.1 = (f32[8,128,128]{2,1,0:T(8,128)S(1)}, f32[8,128,128]{2,1,0:T(8,128)S(1)}, u32[]{:S(2)}, u32[]{:S(2)}) collective-permute-start(f32[8,128,128]{2,1,0:T(8,128)S(1)} %add.62), channel_id=1, source_target_pairs={{0,8},{4,12},{8,16},{12,20},{16,24},{20,28},{24,32},{28,36},{32,40... | collective-permute-start | bytes 1572872 | tf_op jit(solution)/shard_map/ppermute | solution.py:13
  32.6 32.5 %copy-start.6 = (bf16[768,1024]{1,0:T(8,128)(2,1)S(1)}, bf16[768,1024]{1,0:T(8,128)(2,1)}, u32[]{:S(2)}) copy-start(bf16[768,1024]{1,0:T(8,128)(2,1)} %param.6) | copy-start | bytes 4718596
  32.6 13.4 %collective-permute-start.2 = (f32[8,128,128]{2,1,0:T(8,128)S(1)}, f32[8,128,128]{2,1,0:T(8,128)S(1)}, u32[]{:S(2)}, u32[]{:S(2)}) collective-permute-start(f32[8,128,128]{2,1,0:T(8,128)S(1)} %add.63), channel_id=1, source_target_pairs={{0,16},{4,20},{8,24},{12,28},{16,32},{20,36},{24,40},{28,44},{32,4... | collective-permute-start | bytes 1572872 | tf_op jit(solution)/shard_map/ppermute | solution.py:13
  46.1 17.0 %collective-permute-start.3 = (f32[8,128,128]{2,1,0:T(8,128)S(1)}, f32[8,128,128]{2,1,0:T(8,128)S(1)}, u32[]{:S(2)}, u32[]{:S(2)}) collective-permute-start(f32[8,128,128]{2,1,0:T(8,128)S(1)} %add.64), channel_id=1, source_target_pairs={{0,32},{4,36},{8,40},{12,44},{16,48},{20,52},{24,56},{28,60},{32,6... | collective-permute-start | bytes 1572872 | tf_op jit(solution)/shard_map/ppermute | solution.py:13
  63.2 13.8 %collective-permute-start.4 = (f32[8,128,128]{2,1,0:T(8,128)S(1)}, f32[8,128,128]{2,1,0:T(8,128)S(1)}, u32[]{:S(2)}, u32[]{:S(2)}) collective-permute-start(f32[8,128,128]{2,1,0:T(8,128)S(1)} %add.65), channel_id=1, source_target_pairs={{0,64},{4,68},{8,72},{12,76},{16,80},{20,84},{24,88},{28,92},{32,9... | collective-permute-start | bytes 1572872 | tf_op jit(solution)/shard_map/ppermute | solution.py:13
  68.2 18.1 %copy-start.2 = (bf16[8,768,768]{2,1,0:T(8,128)(2,1)}, bf16[8,768,768]{2,1,0:T(8,128)(2,1)S(1)}, u32[]{:S(2)}) copy-start(bf16[8,768,768]{2,1,0:T(8,128)(2,1)S(1)} %select_convert_fusion.1) | copy-start | bytes 28311556
  77.8 34.8 %collective-permute-start.5 = (f32[8,128,128]{2,1,0:T(8,128)}, f32[8,128,128]{2,1,0:T(8,128)}, u32[]{:S(2)}, u32[]{:S(2)}) collective-permute-start(f32[8,128,128]{2,1,0:T(8,128)} %add.66), channel_id=1, source_target_pairs={{0,128},{4,132},{8,136},{12,140},{16,144},{20,148},{24,152},{28,15... | collective-permute-start | bytes 1572872 | tf_op jit(solution)/shard_map/ppermute | solution.py:13
  139.9 35.6 %copy-start.9 = (f32[8,128,128]{1,2,0:T(8,128)}, f32[8,128,128]{1,2,0:T(8,128)S(1)}, u32[]{:S(2)}) copy-start(f32[8,128,128]{1,2,0:T(8,128)S(1)} %fusion.21) | copy-start | bytes 1572868
  139.9 46.2 %copy-start.4 = (bf16[768,1024]{1,0:T(8,128)(2,1)S(1)}, bf16[768,1024]{1,0:T(8,128)(2,1)}, u32[]{:S(2)}) copy-start(bf16[768,1024]{1,0:T(8,128)(2,1)} %param.7) | copy-start | bytes 4718596
  139.9 12.9 %collective-permute-start.6 = (f32[8,128,128]{1,2,0:T(8,128)S(1)}, f32[8,128,128]{1,2,0:T(8,128)S(1)}, u32[]{:S(2)}, u32[]{:S(2)}) collective-permute-start(f32[8,128,128]{1,2,0:T(8,128)S(1)} %fusion.21), channel_id=1, source_target_pairs={{4,0},{8,4},{12,8},{16,12},{20,16},{24,20},{28,24},{32,28},{36,32}... | collective-permute-start | bytes 1572872 | tf_op jit(solution)/shard_map/ppermute | solution.py:13
  152.8 21.8 %collective-permute-start.7 = (f32[8,128,128]{1,2,0:T(8,128)S(1)}, f32[8,128,128]{1,2,0:T(8,128)S(1)}, u32[]{:S(2)}, u32[]{:S(2)}) collective-permute-start(f32[8,128,128]{1,2,0:T(8,128)S(1)} %add.73), channel_id=1, source_target_pairs={{8,0},{12,4},{16,8},{20,12},{24,16},{28,20},{32,24},{36,28},{40,32... | collective-permute-start | bytes 1572872 | tf_op jit(solution)/shard_map/ppermute | solution.py:13
  175.5 20.6 %collective-permute-start.8 = (f32[8,128,128]{1,2,0:T(8,128)}, f32[8,128,128]{1,2,0:T(8,128)}, u32[]{:S(2)}, u32[]{:S(2)}) collective-permute-start(f32[8,128,128]{1,2,0:T(8,128)} %add.74), channel_id=1, source_target_pairs={{16,0},{20,4},{24,8},{28,12},{32,16},{36,20},{40,24},{44,28},{48,3... | collective-permute-start | bytes 1572872 | tf_op jit(solution)/shard_map/ppermute | solution.py:13
  190.2 22.6 %copy-start.1 = (bf16[8,768,768]{2,1,0:T(8,128)(2,1)}, bf16[8,768,768]{2,1,0:T(8,128)(2,1)S(1)}, u32[]{:S(2)}) copy-start(bf16[8,768,768]{2,1,0:T(8,128)(2,1)S(1)} %select_convert_fusion) | copy-start | bytes 28311556
  198.2 20.9 %collective-permute-start.9 = (f32[8,128,128]{1,2,0:T(8,128)}, f32[8,128,128]{1,2,0:T(8,128)}, u32[]{:S(2)}, u32[]{:S(2)}) collective-permute-start(f32[8,128,128]{1,2,0:T(8,128)} %add.75), channel_id=1, source_target_pairs={{32,0},{36,4},{40,8},{44,12},{48,16},{52,20},{56,24},{60,28},{64,3... | collective-permute-start | bytes 1572872 | tf_op jit(solution)/shard_map/ppermute | solution.py:13
  219.0 44.8 %slice-start = ((s8[9437184]{0:T(1024)(128)(4,1)}), s8[4194304]{0:T(1024)(128)(4,1)S(1)}, s32[]{:S(2)}) async-start(s8[9437184]{0:T(1024)(128)(4,1)} %bitcast.101), calls=%async_computation | async-start | bytes 8388608
  220.5 43.4 %slice-start.1 = ((s8[9437184]{0:T(1024)(128)(4,1)}), s8[4194304]{0:T(1024)(128)(4,1)S(1)}, s32[]{:S(2)}) async-start(s8[9437184]{0:T(1024)(128)(4,1)} %bitcast.101), calls=%async_computation.1 | async-start | bytes 8388608
  220.5 43.4 %slice-start.2 = ((s8[9437184]{0:T(1024)(128)(4,1)}), s8[1048576]{0:T(1024)(128)(4,1)S(1)}, s32[]{:S(2)}) async-start(s8[9437184]{0:T(1024)(128)(4,1)} %bitcast.101), calls=%async_computation.2 | async-start | bytes 2097152
  220.5 41.8 %collective-permute-start.10 = (f32[8,128,128]{1,2,0:T(8,128)S(1)}, f32[8,128,128]{1,2,0:T(8,128)S(1)}, u32[]{:S(2)}, u32[]{:S(2)}) collective-permute-start(f32[8,128,128]{1,2,0:T(8,128)S(1)} %add.76), channel_id=1, source_target_pairs={{64,0},{68,4},{72,8},{76,12},{80,16},{84,20},{88,24},{92,28},{96,3... | collective-permute-start | bytes 1572872 | tf_op jit(solution)/shard_map/ppermute | solution.py:13
  262.4 29.0 %copy-start.10 = (f32[8,128,128]{1,2,0:T(8,128)S(1)}, f32[8,128,128]{1,2,0:T(8,128)}, u32[]{:S(2)}) copy-start(f32[8,128,128]{1,2,0:T(8,128)} %copy-done.9) | copy-start | bytes 1572868
  262.4 29.0 %collective-permute-start.11 = (f32[8,128,128]{1,2,0:T(8,128)S(1)}, f32[8,128,128]{1,2,0:T(8,128)S(1)}, u32[]{:S(2)}, u32[]{:S(2)}) collective-permute-start(f32[8,128,128]{1,2,0:T(8,128)S(1)} %add.77), channel_id=1, source_target_pairs={{128,0},{132,4},{136,8},{140,12},{144,16},{148,20},{152,24},{156,2... | collective-permute-start | bytes 1572872 | tf_op jit(solution)/shard_map/ppermute | solution.py:13
  267.1 24.4 %copy-start.7 = (bf16[768,1024]{1,0:T(8,128)(2,1)S(1)}, bf16[768,1024]{1,0:T(8,128)(2,1)}, u32[]{:S(2)}) copy-start(bf16[768,1024]{1,0:T(8,128)(2,1)} %param.6) | copy-start | bytes 4718596
  (4 other events, 23.9 us)
where the time goes:
time: 303 us; the launch traced here: 302 us
  waiting for transfers between devices  152 us (50%)
  starting transfers between devices  62.9 us (21%)
  matrix products  44 us (15%)
  local copies, waits for them, and re-layouts  19.4 us (6%)
  other arithmetic  13.9 us (5%)
  blocking collectives  8.82 us (3%)
    ppermute x12, waiting for transfers between devices, shifted(): return lax.ppermute(block, axis, route)  152 us
    ppermute x12, starting transfers between devices, shifted(): return lax.ppermute(block, axis, route)  62.9 us
    unnamed x36, local copies, waits for them, and re-layouts  11.1 us
    psum x1, blocking collectives, local(): lax.psum((jnp.sum(attention * attention, axis=1), jnp.sum(grad_float * at...  8.82 us
    dot_general x2, matrix products, causal_scores(): jnp.einsum('thi,shi->hts', left, right, preferred_element_type=jnp.float32)  7.2 us
    dot_general x1, matrix products, local(): jnp.einsum('hts,she->the', forward_scores, value_heads, preferred_element...  6.34 us
    dot_general x1, matrix products, local(): jnp.einsum('hts,shi->thi', grad_scores, key_heads, preferred_element_type...  6.21 us
  transfers between devices with their start and end apart: 12, of which 11 were waited for; matrix products, arithmetic and copies ran while one was open for 11% of the time, Pallas kernels for 0%

commit v1 on v0

v1 whole, which is shorter than its diff:
```python
import jax
import jax.numpy as jnp
from jax import lax
from jax.experimental import pallas as pl
from jax.experimental.pallas import tpu as pltpu
from jax.sharding import PartitionSpec as P

HEADS = 32
DH = 128
TOK = 768
HERE = 8
HALF = 4
FEAT = HERE * DH
XS, YS, ZS = 4, 4, 8
SL = DH // ZS
BLK = 256
NBLK = TOK // BLK
F32 = jnp.float32
BF16 = jnp.bfloat16

NN = (((1,), (0,)), ((), ()))
NT = (((1,), (1,)), ((), ()))
TN = (((0,), (0,)), ((), ()))


def mm(a, b, dims):
    return lax.dot_general(a, b, dims, preferred_element_type=F32)


def cols(h):
    return pl.ds(pl.multiple_of(h * DH, DH), DH)


def send(src, dst, ssem, rsem, target):
    return pltpu.make_async_remote_copy(
        src_ref=src,
        dst_ref=dst,
        send_sem=ssem,
        recv_sem=rsem,
        device_id=target,
        device_id_type=pl.DeviceIdType.MESH,
    )


def main_kernel(
    q_hbm, k_hbm, v_hbm, c_hbm, s_hbm,
    out, gq, gkp, gvp, k, v, sfx,
    q, c, s0, sc, dsb, att, d, invb, wb, low, st,
    kv, cr, cs, xr, tt, zt, zp, zr, xp, pr, fs, fr,
    load_sem, cs_sem, cr_sem, xs_sem, xr_sem, zs_sem, zr_sem, ys_sem, yr_sem,
):
    ci = lax.axis_index("ctx")
    y = lax.axis_index("head")
    z = ci // (2 * XS)
    x = (ci // 2) % XS
    core = ci % 2

    def dev(zz, xx, cc, yy):
        return ((zz * XS + xx) * 2 + cc, yy)

    partner = dev(z, x, 1 - core, y)
    x_devs = [dev(z, (x + i) % XS, core, y) for i in range(1, XS)]
    z_devs = [dev((z + i) % ZS, x, core, y) for i in range(1, ZS)]
    y_devs = [dev(z, x, core, (y + i) % YS) for i in range(1, YS)]
    peers = [partner] + x_devs + z_devs + y_devs

    def half_cols(cc):
        return pl.ds(pl.multiple_of(cc * (HALF * DH), HALF * DH), HALF * DH)

    loads = []
    for n, cc in enumerate((1 - core, core)):
        for m, (src, dst) in enumerate(((k_hbm, k), (v_hbm, v))):
            loads.append(
                pltpu.make_async_copy(
                    src.at[:, half_cols(cc)], dst.at[:, half_cols(cc)], load_sem.at[2 * n + m]
                )
            )
    loads.append(pltpu.make_async_copy(q_hbm, q, load_sem.at[4]))
    loads.append(pltpu.make_async_copy(c_hbm, c, load_sem.at[5]))
    loads.append(
        pltpu.make_async_copy(
            s_hbm.at[core * HALF + x, pl.ds(pl.multiple_of(z * SL, SL), SL)], s0, load_sem.at[6]
        )
    )
    for copy in loads:
        copy.start()

    barrier = pltpu.get_barrier_semaphore()
    for peer in peers:
        pl.semaphore_signal(barrier, inc=1, device_id=peer, device_id_type=pl.DeviceIdType.MESH)

    def loop(lo, hi, body):
        def step(i, carry):
            body(i)
            return carry

        lax.fori_loop(lo, hi, step, 0)

    rows_i = lax.broadcasted_iota(jnp.int32, (BLK, BLK), 0)
    cols_i = lax.broadcasted_iota(jnp.int32, (BLK, BLK), 1)

    def scores_into(dst, left, right, h):
        for i in range(NBLK):
            rows = slice(i * BLK, (i + 1) * BLK)
            li = left[rows, cols(h)]
            for j in range(i + 1):
                s = mm(li, right[j * BLK:(j + 1) * BLK, cols(h)], NT)
                if i == j:
                    s = jnp.where(rows_i >= cols_i, s, 0.0)
                dst(rows, slice(j * BLK, (j + 1) * BLK), s.astype(BF16))

    def forward_unit(h):
        def put(rows, columns, val):
            sc[h, rows, columns] = val

        scores_into(put, q, k, h)
        for i in range(NBLK):
            rows = slice(i * BLK, (i + 1) * BLK)
            n = (i + 1) * BLK
            att[rows, cols(h)] = mm(sc[h, rows, 0:n], v[0:n, cols(h)], NN)

    def backward_unit(h):
        def put(rows, columns, val):
            dsb[rows, columns] = val

        scores_into(put, d, v, h)
        for i in range(NBLK):
            rows = slice(i * BLK, (i + 1) * BLK)
            n = (i + 1) * BLK
            g = mm(dsb[rows, 0:n], k[0:n, cols(h)], NN) + mm(d[rows, cols(h)], low[h], NT)
            gq[rows, cols(h)] = g.astype(BF16)
        qt = q[:, cols(h)].T
        dt = d[:, cols(h)].T
        for j in range(NBLK):
            columns = slice(j * BLK, (j + 1) * BLK)
            n = j * BLK
            gkp[columns, cols(h)] = mm(qt[:, n:], dsb[n:, columns], NN).T
            gvp[columns, cols(h)] = mm(dt[:, n:], sc[h, n:, columns], NN).T

    def scan(r, reverse, terms, state, work, done):
        own = core * HALF
        other = (1 - core) * HALF
        def term(j, base):
            kv[r, base + j] = terms(base + j).reshape(ZS, SL, DH)

        loop(0, HALF, lambda j: term(j, other))
        if r == 0:
            pl.semaphore_wait(barrier, len(peers))
        a = send(kv.at[r, pl.ds(other, HALF)], cr.at[r], cs_sem.at[r, 0], cr_sem.at[r, 0], partner)
        a.start()
        if r == 0:
            loads[2].wait()
            loads[3].wait()
        loop(0, HALF, lambda j: term(j, own))
        a.wait_recv()
        cs[r] = kv[r, pl.ds(own, HALF)] + cr[r]
        b = [
            send(cs.at[r, (x + i) % XS], xr.at[r, x], xs_sem.at[r, 0, i - 1], xr_sem.at[r, 0, i - 1], x_devs[i - 1])
            for i in (2, 1, 3)
        ]
        for copy in b:
            copy.start()
        xr[r, x] = cs[r, x]
        work(0)
        for copy in b:
            copy.wait_recv()
        tt[r] = xr[r, 0] + xr[r, 1] + xr[r, 2] + xr[r, 3]
        order = (4, 3, 5, 2, 6, 1, 7)
        e = [
            send(tt.at[r, (z + i) % ZS], zt.at[r, z], zs_sem.at[r, 0, i - 1], zr_sem.at[r, 0, i - 1], z_devs[i - 1])
            for i in order
        ]
        for copy in e:
            copy.start()
        zt[r, z] = tt[r, z]
        work(1)
        for copy in e:
            copy.wait_recv()
        total = state()
        for zz in range(ZS - 1, -1, -1) if reverse else range(ZS):
            zp[r, zz] = total
            total = total + zt[r, zz]
        f = [
            send(zp.at[r, (z + i) % ZS], zr.at[r, z], zs_sem.at[r, 1, i - 1], zr_sem.at[r, 1, i - 1], z_devs[i - 1])
            for i in order
        ]
        for copy in f:
            copy.start()
        zr[r, z] = zp[r, z]
        work(2)
        for copy in f:
            copy.wait_recv()
        total = zr[r]
        for xx in range(XS - 1, -1, -1) if reverse else range(XS):
            xp[r, xx] = total
            total = total + xr[r, xx]
        g = [
            send(xp.at[r, (x + i) % XS], pr.at[r, x], xs_sem.at[r, 1, i - 1], xr_sem.at[r, 1, i - 1], x_devs[i - 1])
            for i in (2, 1, 3)
        ]
        for copy in g:
            copy.start()
        pr[r, x] = xp[r, x]
        work(3)
        for copy in g:
            copy.wait_recv()
        later = core == (0 if reverse else 1)
        fs[r] = pr[r] + jnp.where(later, 0.0, kv[r, pl.ds(own, HALF)])
        o = send(fs.at[r], fr.at[r], cs_sem.at[r, 1], cr_sem.at[r, 1], partner)
        o.start()
        for j in range(HALF):
            done(own + j, (pr[r, j] + jnp.where(later, cr[r, j], 0.0)).reshape(DH, DH))
        o.wait_recv()
        for j in range(HALF):
            done(other + j, fr[r, j].reshape(DH, DH))
        for copy in [a] + b + e + f + g + [o]:
            copy.wait_send()

    loads[0].wait()
    loads[1].wait()

    def forward_term(h):
        return mm(k[:, cols(h)], v[:, cols(h)], TN)

    def forward_work(n):
        if n == 0:
            loads[4].wait()
        if n == 3:
            loads[5].wait()
        loop(2 * n, 2 * n + 2, forward_unit)

    def forward_state():
        loads[6].wait()
        return s0[...]

    def forward_done(h, val):
        low[h] = val.astype(BF16)

    scan(0, False, forward_term, forward_state, forward_work, forward_done)

    st[y] = jnp.zeros((8, TOK), F32)
    for i in range(NBLK):
        rows = slice(i * BLK, (i + 1) * BLK)
        squares = jnp.zeros((BLK, DH), F32)
        cross = jnp.zeros((BLK, DH), F32)
        for h in range(HERE):
            hc = slice(h * DH, (h + 1) * DH)
            a = att[rows, hc] + mm(q[rows, hc], low[h], NN)
            att[rows, hc] = a
            squares = squares + a * a
            cross = cross + a * c[rows, hc].astype(F32)
        st[y, 0:1, rows] = jnp.sum(squares.T, axis=0, keepdims=True)
        st[y, 1:2, rows] = jnp.sum(cross.T, axis=0, keepdims=True)
    stats = [
        send(st.at[y], st.at[y], ys_sem.at[i - 1], yr_sem.at[i - 1], y_devs[i - 1]) for i in (2, 1, 3)
    ]
    for copy in stats:
        copy.start()
    for copy in stats:
        copy.wait()
    total = st[0] + st[1] + st[2] + st[3]
    inv = lax.rsqrt(total[0:1] / (HEADS * DH) + 1e-06)
    weight = inv * inv * inv * total[1:2] / (HEADS * DH)
    invb[...] = jnp.broadcast_to(inv, (DH, TOK)).T
    wb[...] = jnp.broadcast_to(weight, (DH, TOK)).T

    def backward_term(h):
        a = att[:, cols(h)]
        out[:, cols(h)] = (a * invb[...]).astype(BF16)
        dh = (invb[...] * c[:, cols(h)].astype(F32) - a * wb[...]).astype(BF16)
        d[:, cols(h)] = dh
        return mm(q[:, cols(h)], dh, TN)

    def backward_work(n):
        loop(2 * n, 2 * n + 2, backward_unit)

    def backward_done(h, val):
        sfx[h] = val.astype(BF16)

    scan(1, True, backward_term, lambda: jnp.zeros((SL, DH), F32), backward_work, backward_done)


def last_kernel(out_in, gq_in, gkp, gvp, k, v, sfx, out, gq, gk, gv, gkb, gvb, sem):
    first = [
        pltpu.make_async_copy(out_in, out, sem.at[0, 0]),
        pltpu.make_async_copy(gq_in, gq, sem.at[0, 1]),
    ]
    for copy in first:
        copy.start()
    later = []
    for h in range(HERE):
        hc = slice(h * DH, (h + 1) * DH)
        gkb[:, hc] = (gkp[:, hc] + mm(v[:, hc], sfx[h], NT)).astype(BF16)
        gvb[:, hc] = (gvp[:, hc] + mm(k[:, hc], sfx[h], NN)).astype(BF16)
        if h % 2 == 1:
            two = slice((h - 1) * DH, (h + 1) * DH)
            for n, (src, dst) in enumerate(((gkb, gk), (gvb, gv))):
                copy = pltpu.make_async_copy(src.at[:, two], dst.at[:, two], sem.at[1 + h // 2, n])
                copy.start()
                later.append(copy)
    for copy in first + later:
        copy.wait()


def local(queries, keys, values, cotangent, state_in):
    hbm = pl.BlockSpec(memory_space=pltpu.HBM)
    vmem = pl.BlockSpec(memory_space=pltpu.VMEM)
    wide = (TOK, FEAT)
    mid = pl.pallas_call(
        main_kernel,
        name="scan_and_attention",
        out_shape=(
            pltpu.VMEM(wide, BF16),
            pltpu.VMEM(wide, BF16),
            pltpu.VMEM(wide, F32),
            pltpu.VMEM(wide, F32),
            pltpu.VMEM(wide, BF16),
            pltpu.VMEM(wide, BF16),
            pltpu.VMEM((HERE, DH, DH), BF16),
        ),
        in_specs=[hbm] * 5,
        out_specs=(vmem,) * 7,
        scratch_shapes=[
            pltpu.VMEM(wide, BF16),
            pltpu.VMEM(wide, BF16),
            pltpu.VMEM((SL, DH), F32),
            pltpu.VMEM((HERE, TOK, TOK), BF16),
            pltpu.VMEM((TOK, TOK), BF16),
            pltpu.VMEM(wide, F32),
            pltpu.VMEM(wide, BF16),
            pltpu.VMEM((TOK, DH), F32),
            pltpu.VMEM((TOK, DH), F32),
            pltpu.VMEM((HERE, DH, DH), BF16),
            pltpu.VMEM((YS, 8, TOK), F32),
            pltpu.VMEM((2, HERE, ZS, SL, DH), F32),
            pltpu.VMEM((2, HALF, ZS, SL, DH), F32),
            pltpu.VMEM((2, HALF, ZS, SL, DH), F32),
            pltpu.VMEM((2, XS, ZS, SL, DH), F32),
            pltpu.VMEM((2, ZS, SL, DH), F32),
            pltpu.VMEM((2, ZS, SL, DH), F32),
            pltpu.VMEM((2, ZS, SL, DH), F32),
            pltpu.VMEM((2, ZS, SL, DH), F32),
            pltpu.VMEM((2, XS, ZS, SL, DH), F32),
            pltpu.VMEM((2, XS, ZS, SL, DH), F32),
            pltpu.VMEM((2, HALF, ZS, SL, DH), F32),
            pltpu.VMEM((2, HALF, ZS, SL, DH), F32),
            pltpu.SemaphoreType.DMA((7,)),
            pltpu.SemaphoreType.DMA((2, 2)),
            pltpu.SemaphoreType.DMA((2, 2)),
            pltpu.SemaphoreType.DMA((2, 2, XS - 1)),
            pltpu.SemaphoreType.DMA((2, 2, XS - 1)),
            pltpu.SemaphoreType.DMA((2, 2, ZS - 1)),
            pltpu.SemaphoreType.DMA((2, 2, ZS - 1)),
            pltpu.SemaphoreType.DMA((YS - 1,)),
            pltpu.SemaphoreType.DMA((YS - 1,)),
        ],
        compiler_params=pltpu.CompilerParams(
            collective_id=0, has_side_effects=True, vmem_limit_bytes=40 * 2**20
        ),
    )(queries, keys, values, cotangent, state_in)
    return pl.pallas_call(
        last_kernel,
        name="add_states",
        out_shape=(jax.ShapeDtypeStruct(wide, BF16),) * 4,
        in_specs=[vmem] * 7,
        out_specs=(hbm,) * 4,
        scratch_shapes=[
            pltpu.VMEM(wide, BF16),
            pltpu.VMEM(wide, BF16),
            pltpu.SemaphoreType.DMA((5, 2)),
        ],
        compiler_params=pltpu.CompilerParams(vmem_limit_bytes=16 * 2**20),
    )(*mid)


def solution(mesh):
    wide = P("ctx", "head")
    return jax.shard_map(
        local,
        mesh=mesh,
        in_specs=(wide, wide, wide, wide, P("head", None, None)),
        out_specs=(wide, wide, wide, wide),
        check_vma=False,
    )
```

time: 303 us -> 66.3 us (0.22)
  the two profiles are of different devices: /device:TPU:65 before, /device:TPU:1 now
where the time goes in v1:
time: 66.3 us; the launch traced here: 66.2 us
  Pallas kernels  64.5 us (97%)
  local copies, waits for them, and re-layouts  1.03 us (2%)
    pallas_call x1, Pallas kernels, local(): pl.pallas_call(main_kernel, name='scan_and_attention', out_shape=(pltpu.V...  61.8 us
    pallas_call x1, Pallas kernels, local(): pl.pallas_call(last_kernel, name='add_states', out_shape=(jax.ShapeDtypeS...  2.73 us

profile of v1, /device:TPU:1, one launch (start us, length us, event | category | flops | bytes accessed | tf_op | source)
XLA Modules:
  0.0 66.2 jit_solution(808327345089028949)
XLA Ops:
  0.6 0.0 copy-start
  0.6 1.0 %copy-done = f32[8,128,128]{2,1,0:T(8,128)S(1)} copy-done((f32[8,128,128]{2,1,0:T(8,128)S(1)}, f32[8,128,128]{2,1,0:T(8,128)}, u32[]{:S(2)}) %copy-start) | copy-done | bytes 524312
  1.7 61.8 %scan_and_attention.1 = (bf16[768,1024]{1,0:T(8,128)(2,1)S(1)}, bf16[768,1024]{1,0:T(8,128)(2,1)S(1)}, f32[768,1024]{1,0:T(8,128)S(1)}, f32[768,1024]{1,0:T(8,12...) custom-call(bf16[768,1024]{1,0:T(8,128)(2,1)} %q_hbm.1, ...), custom_call_target="tpu_custom_call" | custom-call | tf_op jit(solution)/shard_map/scan_and_attention/pallas_call | solution.py:309
  63.5 2.7 %add_states.1 = (bf16[768,1024]{1,0:T(8,128)(2,1)}, bf16[768,1024]{1,0:T(8,128)(2,1)}, bf16[768,1024]{1,0:T(8,128)(2,1)}, bf16[768,1024]{1,0:T(8,128)(2,1)}) custom-call(bf16[768,1024]{1,0:T(8,128)(2,1)S(1)} %get-tuple-element.11.out_in, bf16[768,1024]{1,0:T(8,128)(2,1)S(1)} %get-tuple-element.12.gq_in, f32[768,1024]{1,0:T(8,128)S(1)} %get-tuple-element.13.gkp, ...), custom_call_target="tpu_custom_call" | custom-call | tf_op jit(solution)/shard_map/add_states/pallas_call | solution.py:361
Async XLA Ops:
  0.6 1.0 %copy-start = (f32[8,128,128]{2,1,0:T(8,128)S(1)}, f32[8,128,128]{2,1,0:T(8,128)}, u32[]{:S(2)}) copy-start(f32[8,128,128]{2,1,0:T(8,128)} %s_hbm.1) | copy-start | bytes 1572868

commit v2 on v1

v2 whole, which is shorter than its diff:
```python
import jax
import jax.numpy as jnp
from jax import lax
from jax.experimental import pallas as pl
from jax.experimental.pallas import tpu as pltpu
from jax.sharding import PartitionSpec as P

HEADS = 32
DH = 128
TOK = 768
HERE = 8
HALF = 4
FEAT = HERE * DH
XS, YS, ZS = 4, 4, 8
CHIPS = XS * ZS
CHUNKS = 2
PAIR = HALF // CHUNKS
SL = PAIR * DH // CHIPS
FORWARD_UNITS = (0, 6, 7, 8, 8)
BACKWARD_UNITS = (0, 4, 5, 7, 8)
BLK = 256
NBLK = TOK // BLK
F32 = jnp.float32
BF16 = jnp.bfloat16

NN = (((1,), (0,)), ((), ()))
NT = (((1,), (1,)), ((), ()))
TN = (((0,), (0,)), ((), ()))


def mm(a, b, dims):
    return lax.dot_general(a, b, dims, preferred_element_type=F32)


def cols(h):
    return pl.ds(pl.multiple_of(h * DH, DH), DH)


def send(src, dst, ssem, rsem, target):
    return pltpu.make_async_remote_copy(
        src_ref=src,
        dst_ref=dst,
        send_sem=ssem,
        recv_sem=rsem,
        device_id=target,
        device_id_type=pl.DeviceIdType.MESH,
    )


def main_kernel(
    q_hbm, k_hbm, v_hbm, c_hbm, s_hbm,
    out, gq, gkp, gvp, k, v, sfx,
    q, c, s0, sc, dsb, att, squares, cross, d, invb, wb, low, st,
    kv, cr, cs, got, back, pr, fs, fr,
    load_sem, cs_sem, cr_sem, fs_sem, fr_sem, ys_sem, yr_sem,
):
    ci = lax.axis_index("ctx")
    y = lax.axis_index("head")
    z = ci // (2 * XS)
    x = (ci // 2) % XS
    core = ci % 2
    chip = z * XS + x

    def dev(chip_index, cc, yy):
        return (chip_index * 2 + cc, yy)

    partner = dev(chip, 1 - core, y)
    others = []
    for dz in (4, 3, 5, 2, 6, 1, 7, 0):
        for dx in (2, 1, 3, 0):
            if dz or dx:
                others.append(((z + dz) % ZS) * XS + (x + dx) % XS)
    y_devs = [dev(chip, core, (y + i) % YS) for i in range(1, YS)]
    peers = [partner] + y_devs + [dev(o, core, y) for o in others]

    def head(half, ck, i=0):
        return half * HALF + ck * PAIR + i

    def pair_cols(half, ck):
        return pl.ds(pl.multiple_of(head(half, ck) * DH, PAIR * DH), PAIR * DH)

    loads = {}

    def load(name, src, dst):
        copy = pltpu.make_async_copy(src, dst, load_sem.at[len(loads)])
        copy.start()
        loads[name] = copy

    for ck in range(CHUNKS):
        for side, half in enumerate((1 - core, core)):
            part = pair_cols(half, ck)
            load(("k", ck, side), k_hbm.at[:, part], k.at[:, part])
            load(("v", ck, side), v_hbm.at[:, part], v.at[:, part])
    load("q", q_hbm, q)
    for ck in range(CHUNKS):
        rows = pl.ds(pl.multiple_of((chip % (CHIPS // PAIR)) * SL, SL), SL)
        load(("s", ck), s_hbm.at[head(core, ck) + chip // (CHIPS // PAIR), rows], s0.at[ck])
    load("c", c_hbm, c)

    barrier = pltpu.get_barrier_semaphore()
    for peer in peers:
        pl.semaphore_signal(barrier, inc=1, device_id=peer, device_id_type=pl.DeviceIdType.MESH)

    def loop(lo, hi, body):
        def step(i, carry):
            body(i)
            return carry

        if hi > lo:
            lax.fori_loop(lo, hi, step, 0)

    rows_i = lax.broadcasted_iota(jnp.int32, (BLK, BLK), 0)
    cols_i = lax.broadcasted_iota(jnp.int32, (BLK, BLK), 1)

    def scores_into(dst, left, right, h):
        for i in range(NBLK):
            rows = slice(i * BLK, (i + 1) * BLK)
            li = left[rows, cols(h)]
            for j in range(i + 1):
                s = mm(li, right[j * BLK:(j + 1) * BLK, cols(h)], NT)
                if i == j:
                    s = jnp.where(rows_i >= cols_i, s, 0.0)
                dst(rows, slice(j * BLK, (j + 1) * BLK), s.astype(BF16))

    def forward_unit(h):
        def put(rows, columns, val):
            sc[h, rows, columns] = val

        scores_into(put, q, k, h)
        for i in range(NBLK):
            rows = slice(i * BLK, (i + 1) * BLK)
            n = (i + 1) * BLK
            att[rows, cols(h)] = mm(sc[h, rows, 0:n], v[0:n, cols(h)], NN)

    def backward_unit(h):
        def put(rows, columns, val):
            dsb[rows, columns] = val

        scores_into(put, d, v, h)
        for i in range(NBLK):
            rows = slice(i * BLK, (i + 1) * BLK)
            n = (i + 1) * BLK
            g = mm(dsb[rows, 0:n], k[0:n, cols(h)], NN) + mm(d[rows, cols(h)], low[h], NT)
            gq[rows, cols(h)] = g.astype(BF16)
        qt = q[:, cols(h)].T
        dt = d[:, cols(h)].T
        for j in range(NBLK):
            columns = slice(j * BLK, (j + 1) * BLK)
            n = j * BLK
            gkp[columns, cols(h)] = mm(qt[:, n:], dsb[n:, columns], NN).T
            gvp[columns, cols(h)] = mm(dt[:, n:], sc[h, n:, columns], NN).T

    def all_to_all(src, dst, which):
        for o in others:
            send(src.at[o], dst.at[chip], fs_sem.at[which], fr_sem.at[which], dev(o, core, y)).start()
        dst[chip] = src[chip]

    def all_of(src, dst, which):
        n = CHIPS - 1
        return send(src.at[0:n], dst.at[0:n], fs_sem.at[which], fr_sem.at[which], partner)

    def scan(r, reverse, ready, term, start, work, done):
        swaps = []
        for ck in range(CHUNKS):
            ready(ck, 0)
            for i in range(PAIR):
                kv[r, 1, ck, i * (CHIPS // PAIR):(i + 1) * (CHIPS // PAIR)] = term(
                    head(1 - core, ck, i)
                ).reshape(CHIPS // PAIR, SL, DH)
            if r == 0 and ck == 0:
                pl.semaphore_wait(barrier, len(peers))
            swap = send(kv.at[r, 1, ck], cr.at[r, ck], cs_sem.at[r, 0, ck], cr_sem.at[r, 0, ck], partner)
            swap.start()
            swaps.append(swap)
            ready(ck, 1)
            for i in range(PAIR):
                kv[r, 0, ck, i * (CHIPS // PAIR):(i + 1) * (CHIPS // PAIR)] = term(
                    head(core, ck, i)
                ).reshape(CHIPS // PAIR, SL, DH)
            swap.wait_recv()
            cs[r, ck] = kv[r, 0, ck] + cr[r, ck]
            all_to_all(cs.at[r, ck], got.at[r, ck], (r, 0, ck))
        work(0)
        for ck in range(CHUNKS):
            all_of(cs.at[r, ck], got.at[r, ck], (r, 0, ck)).wait_recv()
            total = start(ck)
            for o in range(CHIPS - 1, -1, -1) if reverse else range(CHIPS):
                back[r, ck, o] = total
                total = total + got[r, ck, o]
            all_to_all(back.at[r, ck], pr.at[r, ck], (r, 1, ck))
            work(1 + ck)
        later = core == (0 if reverse else 1)
        for ck in range(CHUNKS):
            all_of(back.at[r, ck], pr.at[r, ck], (r, 1, ck)).wait_recv()
            fs[r, ck] = pr[r, ck] + jnp.where(later, 0.0, kv[r, 0, ck])
            swap = send(fs.at[r, ck], fr.at[r, ck], cs_sem.at[r, 1, ck], cr_sem.at[r, 1, ck], partner)
            swap.start()
            swaps.append(swap)
            for i in range(PAIR):
                part = slice(i * (CHIPS // PAIR), (i + 1) * (CHIPS // PAIR))
                val = pr[r, ck, part] + jnp.where(later, cr[r, ck, part], 0.0)
                done(head(core, ck, i), val.reshape(DH, DH))
            if ck == 0:
                work(3)
        for ck in range(CHUNKS):
            swaps[CHUNKS + ck].wait_recv()
            for i in range(PAIR):
                part = slice(i * (CHIPS // PAIR), (i + 1) * (CHIPS // PAIR))
                done(head(1 - core, ck, i), fr[r, ck, part].reshape(DH, DH))
        for swap in swaps:
            swap.wait_send()
        for ck in range(CHUNKS):
            all_of(cs.at[r, ck], got.at[r, ck], (r, 0, ck)).wait_send()
            all_of(back.at[r, ck], pr.at[r, ck], (r, 1, ck)).wait_send()

    def forward_ready(ck, side):
        loads["k", ck, side].wait()
        loads["v", ck, side].wait()

    def forward_term(h):
        return mm(k[:, cols(h)], v[:, cols(h)], TN)

    def forward_start(ck):
        loads["s", ck].wait()
        return s0[ck]

    def forward_work(n):
        if n == 0:
            loads["q"].wait()
            squares[...] = jnp.zeros_like(squares)
            cross[...] = jnp.zeros_like(cross)
        if n == 1:
            loads["c"].wait()
        loop(FORWARD_UNITS[n], FORWARD_UNITS[n + 1], forward_unit)

    def forward_done(h, val):
        state = val.astype(BF16)
        low[h] = state
        for i in range(NBLK):
            rows = slice(i * BLK, (i + 1) * BLK)
            a = att[rows, cols(h)] + mm(q[rows, cols(h)], state, NN)
            att[rows, cols(h)] = a
            squares[rows] += a * a
            cross[rows] += a * c[rows, cols(h)].astype(F32)

    scan(0, False, forward_ready, forward_term, forward_start, forward_work, forward_done)

    st[y] = jnp.zeros((8, TOK), F32)
    st[y, 0:1] = jnp.sum(squares[...].T, axis=0, keepdims=True)
    st[y, 1:2] = jnp.sum(cross[...].T, axis=0, keepdims=True)
    stats = [
        send(st.at[y], st.at[y], ys_sem.at[i - 1], yr_sem.at[i - 1], y_devs[i - 1]) for i in (2, 1, 3)
    ]
    for copy in stats:
        copy.start()
    for copy in stats:
        copy.wait()
    total = st[0] + st[1] + st[2] + st[3]
    inv = lax.rsqrt(total[0:1] / (HEADS * DH) + 1e-06)
    weight = inv * inv * inv * total[1:2] / (HEADS * DH)
    invb[...] = jnp.broadcast_to(inv, (DH, TOK)).T
    wb[...] = jnp.broadcast_to(weight, (DH, TOK)).T

    def backward_term(h):
        a = att[:, cols(h)]
        out[:, cols(h)] = (a * invb[...]).astype(BF16)
        dh = (invb[...] * c[:, cols(h)].astype(F32) - a * wb[...]).astype(BF16)
        d[:, cols(h)] = dh
        return mm(q[:, cols(h)], dh, TN)

    def backward_work(n):
        loop(BACKWARD_UNITS[n], BACKWARD_UNITS[n + 1], backward_unit)

    def backward_done(h, val):
        sfx[h] = val.astype(BF16)

    scan(
        1, True, lambda ck, side: None, backward_term, lambda ck: jnp.zeros((SL, DH), F32),
        backward_work, backward_done,
    )


def last_kernel(out_in, gq_in, gkp, gvp, k, v, sfx, out, gq, gk, gv, gkb, gvb, sem):
    first = [
        pltpu.make_async_copy(out_in, out, sem.at[0, 0]),
        pltpu.make_async_copy(gq_in, gq, sem.at[0, 1]),
    ]
    for copy in first:
        copy.start()
    later = []
    for h in range(HERE):
        hc = slice(h * DH, (h + 1) * DH)
        gkb[:, hc] = (gkp[:, hc] + mm(v[:, hc], sfx[h], NT)).astype(BF16)
        gvb[:, hc] = (gvp[:, hc] + mm(k[:, hc], sfx[h], NN)).astype(BF16)
        if h % 2 == 1:
            two = slice((h - 1) * DH, (h + 1) * DH)
            for n, (src, dst) in enumerate(((gkb, gk), (gvb, gv))):
                copy = pltpu.make_async_copy(src.at[:, two], dst.at[:, two], sem.at[1 + h // 2, n])
                copy.start()
                later.append(copy)
    for copy in first + later:
        copy.wait()


def local(*inputs):
    hbm = pl.BlockSpec(memory_space=pltpu.HBM)
    vmem = pl.BlockSpec(memory_space=pltpu.VMEM)
    wide = (TOK, FEAT)
    sums = (CHUNKS, CHIPS, SL, DH)
    mid = pl.pallas_call(
        main_kernel,
        name="scan_and_attention",
        out_shape=(
            pltpu.VMEM(wide, BF16),
            pltpu.VMEM(wide, BF16),
            pltpu.VMEM(wide, F32),
            pltpu.VMEM(wide, F32),
            pltpu.VMEM(wide, BF16),
            pltpu.VMEM(wide, BF16),
            pltpu.VMEM((HERE, DH, DH), BF16),
        ),
        in_specs=[hbm] * 5,
        out_specs=(vmem,) * 7,
        scratch_shapes=[
            pltpu.VMEM(wide, BF16),
            pltpu.VMEM(wide, BF16),
            pltpu.VMEM((CHUNKS, SL, DH), F32),
            pltpu.VMEM((HERE, TOK, TOK), BF16),
            pltpu.VMEM((TOK, TOK), BF16),
            pltpu.VMEM(wide, F32),
            pltpu.VMEM((TOK, DH), F32),
            pltpu.VMEM((TOK, DH), F32),
            pltpu.VMEM(wide, BF16),
            pltpu.VMEM((TOK, DH), F32),
            pltpu.VMEM((TOK, DH), F32),
            pltpu.VMEM((HERE, DH, DH), BF16),
            pltpu.VMEM((YS, 8, TOK), F32),
            pltpu.VMEM((2, 2) + sums, F32),
            pltpu.VMEM((2,) + sums, F32),
            pltpu.VMEM((2,) + sums, F32),
            pltpu.VMEM((2,) + sums, F32),
            pltpu.VMEM((2,) + sums, F32),
            pltpu.VMEM((2,) + sums, F32),
            pltpu.VMEM((2,) + sums, F32),
            pltpu.VMEM((2,) + sums, F32),
            pltpu.SemaphoreType.DMA((6 * CHUNKS + 2,)),
            pltpu.SemaphoreType.DMA((2, 2, CHUNKS)),
            pltpu.SemaphoreType.DMA((2, 2, CHUNKS)),
            pltpu.SemaphoreType.DMA((2, 2, CHUNKS)),
            pltpu.SemaphoreType.DMA((2, 2, CHUNKS)),
            pltpu.SemaphoreType.DMA((YS - 1,)),
            pltpu.SemaphoreType.DMA((YS - 1,)),
        ],
        compiler_params=pltpu.CompilerParams(
            collective_id=0, has_side_effects=True, vmem_limit_bytes=40 * 2**20
        ),
    )(*(pltpu.with_memory_space_constraint(a, pltpu.HBM) for a in inputs))
    return pl.pallas_call(
        last_kernel,
        name="add_states",
        out_shape=(jax.ShapeDtypeStruct(wide, BF16),) * 4,
        in_specs=[vmem] * 7,
        out_specs=(hbm,) * 4,
        scratch_shapes=[
            pltpu.VMEM(wide, BF16),
            pltpu.VMEM(wide, BF16),
            pltpu.SemaphoreType.DMA((5, 2)),
        ],
        compiler_params=pltpu.CompilerParams(vmem_limit_bytes=16 * 2**20),
    )(*mid)


def solution(mesh):
    wide = P("ctx", "head")
    return jax.shard_map(
        local,
        mesh=mesh,
        in_specs=(wide, wide, wide, wide, P("head", None, None)),
        out_specs=(wide, wide, wide, wide),
        check_vma=False,
    )
```

time: 66.3 us -> 57.8 us (0.87)
  Pallas kernels: 64.5 us -> 56.9 us
  local copies, waits for them, and re-layouts: 1.03 us -> 0 us
    pallas_call x1, Pallas kernels: 61.8 us -> 54.2 us  [local(): pl.pallas_call(main_kernel, name='scan_and_attention', out_shape=(pltpu.V...]
    unnamed x2 -> x0, local copies, waits for them, and re-layouts: 1.03 us -> none
where the time goes in v2:
time: 57.8 us; the launch traced here: 57.7 us
  Pallas kernels  56.9 us (98%)
  between operations  0.8 us (1%)
    pallas_call x1, Pallas kernels, local(): pl.pallas_call(main_kernel, name='scan_and_attention', out_shape=(pltpu.V...  54.2 us
    pallas_call x1, Pallas kernels, local(): pl.pallas_call(last_kernel, name='add_states', out_shape=(jax.ShapeDtypeS...  2.73 us

profile of v2, /device:TPU:1, one launch (start us, length us, event | category | flops | bytes accessed | tf_op | source)
XLA Modules:
  0.0 57.7 jit_solution(1589581595970882880)
XLA Ops:
  0.6 54.2 %scan_and_attention.1 = (bf16[768,1024]{1,0:T(8,128)(2,1)S(1)}, bf16[768,1024]{1,0:T(8,128)(2,1)S(1)}, f32[768,1024]{1,0:T(8,128)S(1)}, f32[768,1024]{1,0:T(8,12...) custom-call(bf16[768,1024]{1,0:T(8,128)(2,1)} %q_hbm.1, ...), custom_call_target="tpu_custom_call" | custom-call | tf_op jit(solution)/shard_map/scan_and_attention/pallas_call | solution.py:310
  54.8 2.7 %add_states.1 = (bf16[768,1024]{1,0:T(8,128)(2,1)}, bf16[768,1024]{1,0:T(8,128)(2,1)}, bf16[768,1024]{1,0:T(8,128)(2,1)}, bf16[768,1024]{1,0:T(8,128)(2,1)}) custom-call(bf16[768,1024]{1,0:T(8,128)(2,1)S(1)} %get-tuple-element.11.out_in, bf16[768,1024]{1,0:T(8,128)(2,1)S(1)} %get-tuple-element.12.gq_in, f32[768,1024]{1,0:T(8,128)S(1)} %get-tuple-element.13.gkp, ...), custom_call_target="tpu_custom_call" | custom-call | tf_op jit(solution)/shard_map/add_states/pallas_call | solution.py:358

commit v3 on v2

--- a/solution.py
+++ b/solution.py
@@ -16,8 +16,12 @@
 CHUNKS = 2
 PAIR = HALF // CHUNKS
 SL = PAIR * DH // CHIPS
+FAR_FIRST = sorted(
+    ((dz, dx) for dz in (4, 3, 5, 2, 6, 1, 7, 0) for dx in (2, 1, 3, 0) if dz or dx),
+    key=lambda p: (-min(p[0], ZS - p[0]) - min(p[1], XS - p[1]), 2 * p[0] > ZS),
+)
 FORWARD_UNITS = (0, 6, 7, 8, 8)
-BACKWARD_UNITS = (0, 4, 5, 7, 8)
+BACKWARD_UNITS = (0, 4, 5, 8, 8)
 BLK = 256
 NBLK = TOK // BLK
 F32 = jnp.float32
@@ -49,8 +53,8 @@
 
 def main_kernel(
     q_hbm, k_hbm, v_hbm, c_hbm, s_hbm,
-    out, gq, gkp, gvp, k, v, sfx,
-    q, c, s0, sc, dsb, att, squares, cross, d, invb, wb, low, st,
+    out, gq, gk, gv, gkp, gvp, k, v, sfx,
+    q, c, s0, qt, sc, dsb, att, squares, cross, d, invb, wb, low, st,
     kv, cr, cs, got, back, pr, fs, fr,
     load_sem, cs_sem, cr_sem, fs_sem, fr_sem, ys_sem, yr_sem,
 ):
@@ -65,13 +69,13 @@
         return (chip_index * 2 + cc, yy)
 
     partner = dev(chip, 1 - core, y)
-    others = []
-    for dz in (4, 3, 5, 2, 6, 1, 7, 0):
-        for dx in (2, 1, 3, 0):
-            if dz or dx:
-                others.append(((z + dz) % ZS) * XS + (x + dx) % XS)
+    others = [((z + dz) % ZS) * XS + (x + dx) % XS for dz, dx in FAR_FIRST]
     y_devs = [dev(chip, core, (y + i) % YS) for i in range(1, YS)]
-    peers = [partner] + y_devs + [dev(o, core, y) for o in others]
+    peers = [dev(o, core, y) for o in others] + y_devs + [partner]
+
+    barrier = pltpu.get_barrier_semaphore()
+    for peer in peers:
+        pl.semaphore_signal(barrier, inc=1, device_id=peer, device_id_type=pl.DeviceIdType.MESH)
 
     def head(half, ck, i=0):
         return half * HALF + ck * PAIR + i
@@ -86,8 +90,8 @@
         copy.start()
         loads[name] = copy
 
-    for ck in range(CHUNKS):
-        for side, half in enumerate((1 - core, core)):
+    for side, half in enumerate((1 - core, core)):
+        for ck in range(CHUNKS):
             part = pair_cols(half, ck)
             load(("k", ck, side), k_hbm.at[:, part], k.at[:, part])
             load(("v", ck, side), v_hbm.at[:, part], v.at[:, part])
@@ -96,10 +100,6 @@
         rows = pl.ds(pl.multiple_of((chip % (CHIPS // PAIR)) * SL, SL), SL)
         load(("s", ck), s_hbm.at[head(core, ck) + chip // (CHIPS // PAIR), rows], s0.at[ck])
     load("c", c_hbm, c)
-
-    barrier = pltpu.get_barrier_semaphore()
-    for peer in peers:
-        pl.semaphore_signal(barrier, inc=1, device_id=peer, device_id_type=pl.DeviceIdType.MESH)
 
     def loop(lo, hi, body):
         def step(i, carry):
@@ -126,6 +126,7 @@
         def put(rows, columns, val):
             sc[h, rows, columns] = val
 
+        qt[h] = q[:, cols(h)].T
         scores_into(put, q, k, h)
         for i in range(NBLK):
             rows = slice(i * BLK, (i + 1) * BLK)
@@ -136,18 +137,18 @@
         def put(rows, columns, val):
             dsb[rows, columns] = val
 
+        out[:, cols(h)] = (att[:, cols(h)] * invb[...]).astype(BF16)
         scores_into(put, d, v, h)
         for i in range(NBLK):
             rows = slice(i * BLK, (i + 1) * BLK)
             n = (i + 1) * BLK
             g = mm(dsb[rows, 0:n], k[0:n, cols(h)], NN) + mm(d[rows, cols(h)], low[h], NT)
             gq[rows, cols(h)] = g.astype(BF16)
-        qt = q[:, cols(h)].T
         dt = d[:, cols(h)].T
         for j in range(NBLK):
             columns = slice(j * BLK, (j + 1) * BLK)
             n = j * BLK
-            gkp[columns, cols(h)] = mm(qt[:, n:], dsb[n:, columns], NN).T
+            gkp[columns, cols(h)] = mm(qt[h, :, n:], dsb[n:, columns], NN).T
             gvp[columns, cols(h)] = mm(dt[:, n:], sc[h, n:, columns], NN).T
 
     def all_to_all(src, dst, which):
@@ -160,24 +161,24 @@
         return send(src.at[0:n], dst.at[0:n], fs_sem.at[which], fr_sem.at[which], partner)
 
     def scan(r, reverse, ready, term, start, work, done):
+        def terms(side, half, ck):
+            for i in range(PAIR):
+                part = slice(i * (CHIPS // PAIR), (i + 1) * (CHIPS // PAIR))
+                kv[r, side, ck, part] = term(head(half, ck, i)).reshape(CHIPS // PAIR, SL, DH)
+
         swaps = []
         for ck in range(CHUNKS):
             ready(ck, 0)
-            for i in range(PAIR):
-                kv[r, 1, ck, i * (CHIPS // PAIR):(i + 1) * (CHIPS // PAIR)] = term(
-                    head(1 - core, ck, i)
-                ).reshape(CHIPS // PAIR, SL, DH)
+            terms(1, 1 - core, ck)
             if r == 0 and ck == 0:
                 pl.semaphore_wait(barrier, len(peers))
             swap = send(kv.at[r, 1, ck], cr.at[r, ck], cs_sem.at[r, 0, ck], cr_sem.at[r, 0, ck], partner)
             swap.start()
             swaps.append(swap)
+        for ck in range(CHUNKS):
             ready(ck, 1)
-            for i in range(PAIR):
-                kv[r, 0, ck, i * (CHIPS // PAIR):(i + 1) * (CHIPS // PAIR)] = term(
-                    head(core, ck, i)
-                ).reshape(CHIPS // PAIR, SL, DH)
-            swap.wait_recv()
+            terms(0, core, ck)
+            swaps[ck].wait_recv()
             cs[r, ck] = kv[r, 0, ck] + cr[r, ck]
             all_to_all(cs.at[r, ck], got.at[r, ck], (r, 0, ck))
         work(0)
@@ -196,17 +197,15 @@
             swap = send(fs.at[r, ck], fr.at[r, ck], cs_sem.at[r, 1, ck], cr_sem.at[r, 1, ck], partner)
             swap.start()
             swaps.append(swap)
-            for i in range(PAIR):
-                part = slice(i * (CHIPS // PAIR), (i + 1) * (CHIPS // PAIR))
+            parts = [slice(i * (CHIPS // PAIR), (i + 1) * (CHIPS // PAIR)) for i in range(PAIR)]
+            for i, part in enumerate(parts):
                 val = pr[r, ck, part] + jnp.where(later, cr[r, ck, part], 0.0)
-                done(head(core, ck, i), val.reshape(DH, DH))
+                done(head(core, ck, i), val.reshape(DH, DH), False)
             if ck == 0:
                 work(3)
-        for ck in range(CHUNKS):
-            swaps[CHUNKS + ck].wait_recv()
-            for i in range(PAIR):
-                part = slice(i * (CHIPS // PAIR), (i + 1) * (CHIPS // PAIR))
-                done(head(1 - core, ck, i), fr[r, ck, part].reshape(DH, DH))
+            swap.wait_recv()
+            for i, part in enumerate(parts):
+                done(head(1 - core, ck, i), fr[r, ck, part].reshape(DH, DH), ck == CHUNKS - 1)
         for swap in swaps:
             swap.wait_send()
         for ck in range(CHUNKS):
@@ -233,7 +232,7 @@
             loads["c"].wait()
         loop(FORWARD_UNITS[n], FORWARD_UNITS[n + 1], forward_unit)
 
-    def forward_done(h, val):
+    def forward_done(h, val, last):
         state = val.astype(BF16)
         low[h] = state
         for i in range(NBLK):
@@ -245,7 +244,6 @@
 
     scan(0, False, forward_ready, forward_term, forward_start, forward_work, forward_done)
 
-    st[y] = jnp.zeros((8, TOK), F32)
     st[y, 0:1] = jnp.sum(squares[...].T, axis=0, keepdims=True)
     st[y, 1:2] = jnp.sum(cross[...].T, axis=0, keepdims=True)
     stats = [
@@ -254,7 +252,7 @@
     for copy in stats:
         copy.start()
     for copy in stats:
-        copy.wait()
+        copy.wait_recv()
     total = st[0] + st[1] + st[2] + st[3]
     inv = lax.rsqrt(total[0:1] / (HEADS * DH) + 1e-06)
     weight = inv * inv * inv * total[1:2] / (HEADS * DH)
@@ -263,43 +261,55 @@
 
     def backward_term(h):
         a = att[:, cols(h)]
-        out[:, cols(h)] = (a * invb[...]).astype(BF16)
         dh = (invb[...] * c[:, cols(h)].astype(F32) - a * wb[...]).astype(BF16)
         d[:, cols(h)] = dh
-        return mm(q[:, cols(h)], dh, TN)
+        return mm(qt[h], dh, NN)
 
     def backward_work(n):
         loop(BACKWARD_UNITS[n], BACKWARD_UNITS[n + 1], backward_unit)
 
-    def backward_done(h, val):
-        sfx[h] = val.astype(BF16)
+    def backward_done(h, val, last):
+        state = val.astype(BF16)
+        if last:
+            sfx[h] = state
+        else:
+            gk[:, cols(h)] = (gkp[:, cols(h)] + mm(v[:, cols(h)], state, NT)).astype(BF16)
+            gv[:, cols(h)] = (gvp[:, cols(h)] + mm(k[:, cols(h)], state, NN)).astype(BF16)
 
     scan(
         1, True, lambda ck, side: None, backward_term, lambda ck: jnp.zeros((SL, DH), F32),
         backward_work, backward_done,
     )
-
-
-def last_kernel(out_in, gq_in, gkp, gvp, k, v, sfx, out, gq, gk, gv, gkb, gvb, sem):
-    first = [
-        pltpu.make_async_copy(out_in, out, sem.at[0, 0]),
-        pltpu.make_async_copy(gq_in, gq, sem.at[0, 1]),
-    ]
-    for copy in first:
-        copy.start()
-    later = []
-    for h in range(HERE):
-        hc = slice(h * DH, (h + 1) * DH)
-        gkb[:, hc] = (gkp[:, hc] + mm(v[:, hc], sfx[h], NT)).astype(BF16)
-        gvb[:, hc] = (gvp[:, hc] + mm(k[:, hc], sfx[h], NN)).astype(BF16)
-        if h % 2 == 1:
-            two = slice((h - 1) * DH, (h + 1) * DH)
-            for n, (src, dst) in enumerate(((gkb, gk), (gvb, gv))):
-                copy = pltpu.make_async_copy(src.at[:, two], dst.at[:, two], sem.at[1 + h // 2, n])
-                copy.start()
-                later.append(copy)
-    for copy in first + later:
-        copy.wait()
+    for copy in stats:
+        copy.wait_send()
+
+
+def last_kernel(out_in, gq_in, gk_in, gv_in, gkp, gvp, k, v, sfx, out, gq, gk, gv, gkb, gvb, sem):
+    core = lax.axis_index("ctx") % 2
+    own = pl.ds(pl.multiple_of(core * HALF * DH, HALF * DH), HALF * DH)
+    head = (1 - core) * HALF
+    early = pl.ds(pl.multiple_of(head * DH, PAIR * DH), PAIR * DH)
+    late = pl.ds(pl.multiple_of((head + PAIR) * DH, PAIR * DH), PAIR * DH)
+    copies = []
+
+    def copy(src, dst):
+        copies.append(pltpu.make_async_copy(src, dst, sem.at[len(copies)]))
+        copies[-1].start()
+
+    copy(out_in, out)
+    copy(gq_in, gq)
+    for part in (own, early):
+        copy(gk_in.at[:, part], gk.at[:, part])
+        copy(gv_in.at[:, part], gv.at[:, part])
+    for i in range(PAIR):
+        h = head + PAIR + i
+        here = slice(i * DH, (i + 1) * DH)
+        gkb[:, here] = (gkp[:, cols(h)] + mm(v[:, cols(h)], sfx[h], NT)).astype(BF16)
+        gvb[:, here] = (gvp[:, cols(h)] + mm(k[:, cols(h)], sfx[h], NN)).astype(BF16)
+    copy(gkb, gk.at[:, late])
+    copy(gvb, gv.at[:, late])
+    for c in copies:
+        c.wait()
 
 
 def local(*inputs):
@@ -313,6 +323,8 @@
         out_shape=(
             pltpu.VMEM(wide, BF16),
             pltpu.VMEM(wide, BF16),
+            pltpu.VMEM(wide, BF16),
+            pltpu.VMEM(wide, BF16),
             pltpu.VMEM(wide, F32),
             pltpu.VMEM(wide, F32),
             pltpu.VMEM(wide, BF16),
@@ -320,11 +332,12 @@
             pltpu.VMEM((HERE, DH, DH), BF16),
         ),
         in_specs=[hbm] * 5,
-        out_specs=(vmem,) * 7,
+        out_specs=(vmem,) * 9,
         scratch_shapes=[
             pltpu.VMEM(wide, BF16),
             pltpu.VMEM(wide, BF16),
             pltpu.VMEM((CHUNKS, SL, DH), F32),
+            pltpu.VMEM((HERE, DH, TOK), BF16),
             pltpu.VMEM((HERE, TOK, TOK), BF16),
             pltpu.VMEM((TOK, TOK), BF16),
             pltpu.VMEM(wide, F32),
@@ -334,7 +347,7 @@
             pltpu.VMEM((TOK, DH), F32),
             pltpu.VMEM((TOK, DH), F32),
             pltpu.VMEM((HERE, DH, DH), BF16),
-            pltpu.VMEM((YS, 8, TOK), F32),
+            pltpu.VMEM((YS, 2, TOK), F32),
             pltpu.VMEM((2, 2) + sums, F32),
             pltpu.VMEM((2,) + sums, F32),
             pltpu.VMEM((2,) + sums, F32),
@@ -359,12 +372,12 @@
         last_kernel,
         name="add_states",
         out_shape=(jax.ShapeDtypeStruct(wide, BF16),) * 4,
-        in_specs=[vmem] * 7,
+        in_specs=[vmem] * 9,
         out_specs=(hbm,) * 4,
         scratch_shapes=[
-            pltpu.VMEM(wide, BF16),
-            pltpu.VMEM(wide, BF16),
-            pltpu.SemaphoreType.DMA((5, 2)),
+            pltpu.VMEM((TOK, PAIR * DH), BF16),
+            pltpu.VMEM((TOK, PAIR * DH), BF16),
+            pltpu.SemaphoreType.DMA((8,)),
         ],
         compiler_params=pltpu.CompilerParams(vmem_limit_bytes=16 * 2**20),
     )(*mid)

time: 57.8 us -> 56.9 us (0.984)
  Pallas kernels: 56.9 us -> 56 us
    pallas_call x1, Pallas kernels: 54.2 us -> 53.2 us  [local(): pl.pallas_call(main_kernel, name='scan_and_attention', out_shape=(pltpu.V...]
where the time goes in v3:
time: 56.9 us; the launch traced here: 56.8 us
  Pallas kernels  56 us (98%)
  between operations  0.8 us (1%)
    pallas_call x1, Pallas kernels, local(): pl.pallas_call(main_kernel, name='scan_and_attention', out_shape=(pltpu.V...  53.2 us
    pallas_call x1, Pallas kernels, local(): pl.pallas_call(last_kernel, name='add_states', out_shape=(jax.ShapeDtypeS...  2.76 us

profile of v3, /device:TPU:1, one launch (start us, length us, event | category | flops | bytes accessed | tf_op | source)
XLA Modules:
  0.0 56.8 jit_solution(13466967996136985013)
XLA Ops:
  0.6 53.2 %scan_and_attention.1 = (bf16[768,1024]{1,0:T(8,128)(2,1)S(1)}, bf16[768,1024]{1,0:T(8,128)(2,1)S(1)}, bf16[768,1024]{1,0:T(8,128)(2,1)S(1)}, bf16[768,1024]{1,0...) custom-call(bf16[768,1024]{1,0:T(8,128)(2,1)} %q_hbm.1, ...), custom_call_target="tpu_custom_call" | custom-call | tf_op jit(solution)/shard_map/scan_and_attention/pallas_call | solution.py:320
  53.9 2.8 %add_states.1 = (bf16[768,1024]{1,0:T(8,128)(2,1)}, bf16[768,1024]{1,0:T(8,128)(2,1)}, bf16[768,1024]{1,0:T(8,128)(2,1)}, bf16[768,1024]{1,0:T(8,128)(2,1)}) custom-call(bf16[768,1024]{1,0:T(8,128)(2,1)S(1)} %get-tuple-element.13.out_in, bf16[768,1024]{1,0:T(8,128)(2,1)S(1)} %get-tuple-element.14.gq_in, bf16[768,1024]{1,0:T(8,128)(2,1)S(1)} %get-tuple-element.15.gk_in, ...), custom_call_target="tpu_custom_call" | custom-call | tf_op jit(solution)/shard_map/add_states/pallas_call | solution.py:371

commit v4 on v3

--- a/solution.py
+++ b/solution.py
@@ -167,7 +167,8 @@
                 kv[r, side, ck, part] = term(head(half, ck, i)).reshape(CHIPS // PAIR, SL, DH)
 
         swaps = []
-        for ck in range(CHUNKS):
+
+        def first(ck):
             ready(ck, 0)
             terms(1, 1 - core, ck)
             if r == 0 and ck == 0:
@@ -175,12 +176,18 @@
             swap = send(kv.at[r, 1, ck], cr.at[r, ck], cs_sem.at[r, 0, ck], cr_sem.at[r, 0, ck], partner)
             swap.start()
             swaps.append(swap)
-        for ck in range(CHUNKS):
+
+        def second(ck):
             ready(ck, 1)
             terms(0, core, ck)
             swaps[ck].wait_recv()
             cs[r, ck] = kv[r, 0, ck] + cr[r, ck]
             all_to_all(cs.at[r, ck], got.at[r, ck], (r, 0, ck))
+
+        if r == 0:
+            first(0), first(1), second(0), second(1)
+        else:
+            first(0), second(0), first(1), second(1)
         work(0)
         for ck in range(CHUNKS):
             all_of(cs.at[r, ck], got.at[r, ck], (r, 0, ck)).wait_recv()

time: 56.9 us -> 56.5 us (level)
  no operation moved by 1% of the time
where the time goes in v4:
time: 56.5 us; the launch traced here: 56.4 us
  Pallas kernels  55.6 us (98%)
  between operations  0.8 us (1%)
    pallas_call x1, Pallas kernels, local(): pl.pallas_call(main_kernel, name='scan_and_attention', out_shape=(pltpu.V...  52.8 us
    pallas_call x1, Pallas kernels, local(): pl.pallas_call(last_kernel, name='add_states', out_shape=(jax.ShapeDtypeS...  2.76 us

profile of v4, /device:TPU:1, one launch (start us, length us, event | category | flops | bytes accessed | tf_op | source)
XLA Modules:
  0.0 56.4 jit_solution(11783517919050847814)
XLA Ops:
  0.6 52.8 %scan_and_attention.1 = (bf16[768,1024]{1,0:T(8,128)(2,1)S(1)}, bf16[768,1024]{1,0:T(8,128)(2,1)S(1)}, bf16[768,1024]{1,0:T(8,128)(2,1)S(1)}, bf16[768,1024]{1,0...) custom-call(bf16[768,1024]{1,0:T(8,128)(2,1)} %q_hbm.1, ...), custom_call_target="tpu_custom_call" | custom-call | tf_op jit(solution)/shard_map/scan_and_attention/pallas_call | solution.py:327
  53.5 2.8 %add_states.1 = (bf16[768,1024]{1,0:T(8,128)(2,1)}, bf16[768,1024]{1,0:T(8,128)(2,1)}, bf16[768,1024]{1,0:T(8,128)(2,1)}, bf16[768,1024]{1,0:T(8,128)(2,1)}) custom-call(bf16[768,1024]{1,0:T(8,128)(2,1)S(1)} %get-tuple-element.13.out_in, bf16[768,1024]{1,0:T(8,128)(2,1)S(1)} %get-tuple-element.14.gq_in, bf16[768,1024]{1,0:T(8,128)(2,1)S(1)} %get-tuple-element.15.gk_in, ...), custom_call_target="tpu_custom_call" | custom-call | tf_op jit(solution)/shard_map/add_states/pallas_call | solution.py:378
